TPU v7x, 128 devices: a whole 4x4x4 slice. The times are simulated.
128 devices in a mesh: site: 8 (over y, x_hi), op: 16 (over x_lo, z, core).
Axes of the slice: x: 4 (x_hi: 2, x_lo: 2; x = x_hi * 2 + x_lo), y: 4, z: 4, core: 2. Of those that a mesh axis runs over, the one named last changes fastest.
Arguments:
- mps: bfloat16 [8, 4, 4, 16, 128, 128], P('site'), may hold values from -0.4375 to 0.4375
- sector_map: int32 [8, 4, 16], P('site'), may hold values from 0 to 15, each once within a row
- live_rows: int32 [8, 16], P('site'), may hold values from 32 to 128, as said below
- term_mask: int32 [8, 32, 4], P('site', 'op'), may hold values 0 or 1
- term_coef: float32 [8, 32, 4], P('site', 'op'), may hold values from 0.8 to 2
- block_coef: float32 [8, 32], P('site', 'op'), may hold values from -1.2 to 1.2
- env_terms: bfloat16 [4, 32, 16, 128, 128], P(None, 'op'), may hold values from -6 to 6
- env_block: bfloat16 [4, 16, 128, 128], P(None, None, 'op'), may hold values from -6 to 6
Outputs:
- out_terms: bfloat16 [8, 4, 32, 16, 128, 128], P('site', None, 'op')
- out_block: bfloat16 [8, 4, 16, 128, 128], P('site', None, None, 'op')
Inputs may be any that keep to these rules, and one draw needn't show every extreme that they name: `sector_map`: each row along the last dimension is a permutation of the 16 sectors. `live_rows`: every site has a sector with all 128 states live.
All inputs are finite; a program needn't handle non-finite values. No bound on the sum of `term_mask` on one device may be relied on, other than what follows from the above.
Results may differ from a plain program's by a relative error of at most 0.034.
Values may be sent and summed in bfloat16 or wider, within the bound.
A program may use at most 192 MiB of HBM per device.

v0:
```python
import jax
import jax.numpy as jnp
from jax import lax
from jax.sharding import PartitionSpec as P


def shifted(x, axis, by):
    count = lax.axis_size(axis)
    pairs = [(i, i + by) for i in range(count) if 0 <= i + by < count]
    return lax.ppermute(x, axis, pairs)


def advance_terms(terms, amat, weights, sector_rows):
    source = jnp.take(terms, sector_rows, axis=1)
    product = jnp.einsum("ksrab,srbc->ksrac", source, amat, preferred_element_type=jnp.float32)
    scaled = (product * weights[:, :, None, None, None]).astype(jnp.bfloat16)
    return jnp.einsum("srab,ksrac->krbc", amat, scaled, preferred_element_type=jnp.float32)


def carry_block(block, amat, bra_rows, sector_rows):
    feed = jnp.take(block, sector_rows, axis=0)
    moved = jnp.einsum("srab,srbc->srac", feed, amat, preferred_element_type=jnp.float32).astype(
        jnp.bfloat16
    )
    return jnp.einsum("srab,srac->rbc", bra_rows, moved, preferred_element_type=jnp.float32)


def shards(mps, sector_map, live_rows, term_mask, term_coef, block_coef, env_terms, env_block):
    n_site = lax.axis_size("site")
    place = lax.axis_index("site")
    n_op = lax.axis_size("op")
    rank = lax.axis_index("op")
    roots = env_terms.shape[0]
    width = mps.shape[-1]
    share = width // n_op
    columns = lax.broadcasted_iota(jnp.int32, (1, 1, width), 2)
    local_weights = term_coef * term_mask.astype(jnp.float32)
    start_block = lax.all_gather(env_block, "op", axis=2, tiled=True)
    keep = columns < live_rows[0][:, None, None]
    weights = local_weights[0]
    pair_coef = block_coef[0]
    sector_rows = sector_map[0]
    tensors = mps[0]
    out_terms = jnp.zeros_like(env_terms)
    out_block = jnp.zeros_like(env_block)
    initial = (jnp.zeros_like(env_terms[0]), jnp.zeros_like(start_block[0]), out_terms, out_block)

    def section(step, carry):
        passed_terms, passed_block, out_terms, out_block = carry
        first = jnp.minimum(step, roots - 1)
        terms = jnp.where(
            place == 0, lax.dynamic_index_in_dim(env_terms, first, 0, False), passed_terms
        )
        block = jnp.where(
            place == 0, lax.dynamic_index_in_dim(start_block, first, 0, False), passed_block
        )
        root = step - place
        valid = jnp.logical_and(root >= 0, root < roots)
        slot = jnp.clip(root, 0, roots - 1)
        raw = lax.dynamic_index_in_dim(tensors, slot, 0, False)
        amat = jnp.where(keep, raw, jnp.zeros_like(raw))
        mixed = advance_terms(terms, amat, weights, sector_rows)
        partial_value = jnp.einsum("k,krbc->rbc", pair_coef, mixed)
        new_terms = mixed.astype(jnp.bfloat16)
        own = carry_block(block, amat, amat, sector_rows)
        new_block = (
            own + lax.psum(partial_value.astype(jnp.bfloat16), "op").astype(jnp.float32)
        ).astype(jnp.bfloat16)
        kept = lax.dynamic_slice_in_dim(new_block, rank * share, share, 1)
        old_terms = lax.dynamic_index_in_dim(out_terms, slot, 0, False)
        old_block = lax.dynamic_index_in_dim(out_block, slot, 0, False)
        out_terms = lax.dynamic_update_index_in_dim(
            out_terms, jnp.where(valid, new_terms, old_terms), slot, 0
        )
        out_block = lax.dynamic_update_index_in_dim(
            out_block, jnp.where(valid, kept, old_block), slot, 0
        )
        next_terms, next_block = shifted((new_terms, new_block), "site", 1)
        return (next_terms, next_block, out_terms, out_block)

    final = lax.fori_loop(0, n_site + roots - 1, section, initial)
    return (final[2][None], final[3][None])


def solution(mesh):
    in_specs = (
        P("site", None, None, None, None, None),
        P("site", None, None),
        P("site", None),
        P("site", "op", None),
        P("site", "op", None),
        P("site", "op"),
        P(None, "op", None, None, None),
        P(None, None, "op", None),
    )
    out_specs = (P("site", None, "op", None, None, None), P("site", None, None, "op", None))
    return jax.shard_map(shards, mesh=mesh, in_specs=in_specs, out_specs=out_specs, check_vma=False)
```

profile of v0, /device:TPU:28, one launch (start us, length us, event | category | flops | bytes accessed | tf_op | source)
XLA Modules:
  0.0 1787.0 jit_solution(4495859496122887533)
XLA Ops:
  19.4 29.5 %all-gather.2.cloned.1.call-done = bf16[4,16,128,128]{3,2,1,0:T(8,128)(2,1)} async-done(((bf16[4,16,8,128]{3,2,1,0:T(8,128)(2,1)}), bf16[4,16,128,128]{3,2,1,0:T(8,128)(2,1)}) %all-gather.2.cloned.1.call-update) | async-done | bytes 2097168 | tf_op jit(solution)/shard_map/all_gather | solution.py:38
  54.2 1725.4 %while.22 = (s32[]{:T(128)}, bf16[2,16,128,128]{2,3,0,1:T(8,128)(2,1)}, bf16[16,128,128]{2,1,0:T(8,128)(2,1)}, bf16[4,2,16,128,128]{4,3,2,1,0:T(8,128)(2,1)}, bf...) while((s32[]{:T(128)}, ...), condition=%wide.region_2.3_spmd.clone, body=%wide.region_0.2_spmd.clone.sunk | while | flops 1626885760 | bytes 65196588 | solution.py:81
  76.5 112.9 %all-reduce.2.cloned.1.call-done = bf16[16,128,128]{2,1,0:T(8,128)(2,1)} async-done(((bf16[16,128,128]{2,1,0:T(8,128)(2,1)}), bf16[16,128,128]{2,1,0:T(8,128)(2,1)}) %all-reduce.2.cloned.1.call-update) | async-done | bytes 524304 | tf_op jit(solution)/shard_map/while/body/eval_jaxpr/psum | solution.py:67
  199.3 13.4 collective-permute-done.1
  235.0 111.1 %all-reduce.2.cloned.1.call-done = bf16[16,128,128]{2,1,0:T(8,128)(2,1)} async-done(((bf16[16,128,128]{2,1,0:T(8,128)(2,1)}), bf16[16,128,128]{2,1,0:T(8,128)(2,1)}) %all-reduce.2.cloned.1.call-update) | async-done | bytes 524304 | tf_op jit(solution)/shard_map/while/body/eval_jaxpr/psum | solution.py:67
  355.9 13.4 collective-permute-done.1
  391.6 111.1 %all-reduce.2.cloned.1.call-done = bf16[16,128,128]{2,1,0:T(8,128)(2,1)} async-done(((bf16[16,128,128]{2,1,0:T(8,128)(2,1)}), bf16[16,128,128]{2,1,0:T(8,128)(2,1)}) %all-reduce.2.cloned.1.call-update) | async-done | bytes 524304 | tf_op jit(solution)/shard_map/while/body/eval_jaxpr/psum | solution.py:67
  512.6 13.4 collective-permute-done.1
  548.3 111.1 %all-reduce.2.cloned.1.call-done = bf16[16,128,128]{2,1,0:T(8,128)(2,1)} async-done(((bf16[16,128,128]{2,1,0:T(8,128)(2,1)}), bf16[16,128,128]{2,1,0:T(8,128)(2,1)}) %all-reduce.2.cloned.1.call-update) | async-done | bytes 524304 | tf_op jit(solution)/shard_map/while/body/eval_jaxpr/psum | solution.py:67
  669.3 13.4 collective-permute-done.1
  705.0 111.1 %all-reduce.2.cloned.1.call-done = bf16[16,128,128]{2,1,0:T(8,128)(2,1)} async-done(((bf16[16,128,128]{2,1,0:T(8,128)(2,1)}), bf16[16,128,128]{2,1,0:T(8,128)(2,1)}) %all-reduce.2.cloned.1.call-update) | async-done | bytes 524304 | tf_op jit(solution)/shard_map/while/body/eval_jaxpr/psum | solution.py:67
  825.9 13.4 collective-permute-done.1
  861.6 111.1 %all-reduce.2.cloned.1.call-done = bf16[16,128,128]{2,1,0:T(8,128)(2,1)} async-done(((bf16[16,128,128]{2,1,0:T(8,128)(2,1)}), bf16[16,128,128]{2,1,0:T(8,128)(2,1)}) %all-reduce.2.cloned.1.call-update) | async-done | bytes 524304 | tf_op jit(solution)/shard_map/while/body/eval_jaxpr/psum | solution.py:67
  982.6 13.4 collective-permute-done.1
  1018.3 111.1 %all-reduce.2.cloned.1.call-done = bf16[16,128,128]{2,1,0:T(8,128)(2,1)} async-done(((bf16[16,128,128]{2,1,0:T(8,128)(2,1)}), bf16[16,128,128]{2,1,0:T(8,128)(2,1)}) %all-reduce.2.cloned.1.call-update) | async-done | bytes 524304 | tf_op jit(solution)/shard_map/while/body/eval_jaxpr/psum | solution.py:67
  1139.2 13.4 collective-permute-done.1
  1174.9 111.1 %all-reduce.2.cloned.1.call-done = bf16[16,128,128]{2,1,0:T(8,128)(2,1)} async-done(((bf16[16,128,128]{2,1,0:T(8,128)(2,1)}), bf16[16,128,128]{2,1,0:T(8,128)(2,1)}) %all-reduce.2.cloned.1.call-update) | async-done | bytes 524304 | tf_op jit(solution)/shard_map/while/body/eval_jaxpr/psum | solution.py:67
  1295.9 13.4 collective-permute-done.1
  1331.5 111.3 %all-reduce.2.cloned.1.call-done = bf16[16,128,128]{2,1,0:T(8,128)(2,1)} async-done(((bf16[16,128,128]{2,1,0:T(8,128)(2,1)}), bf16[16,128,128]{2,1,0:T(8,128)(2,1)}) %all-reduce.2.cloned.1.call-update) | async-done | bytes 524304 | tf_op jit(solution)/shard_map/while/body/eval_jaxpr/psum | solution.py:67
  1452.8 13.4 collective-permute-done.1
  1488.4 111.2 %all-reduce.2.cloned.1.call-done = bf16[16,128,128]{2,1,0:T(8,128)(2,1)} async-done(((bf16[16,128,128]{2,1,0:T(8,128)(2,1)}), bf16[16,128,128]{2,1,0:T(8,128)(2,1)}) %all-reduce.2.cloned.1.call-update) | async-done | bytes 524304 | tf_op jit(solution)/shard_map/while/body/eval_jaxpr/psum | solution.py:67
  1609.5 13.4 collective-permute-done.1
  1645.2 111.1 %all-reduce.2.cloned.1.call-done = bf16[16,128,128]{2,1,0:T(8,128)(2,1)} async-done(((bf16[16,128,128]{2,1,0:T(8,128)(2,1)}), bf16[16,128,128]{2,1,0:T(8,128)(2,1)}) %all-reduce.2.cloned.1.call-update) | async-done | bytes 524304 | tf_op jit(solution)/shard_map/while/body/eval_jaxpr/psum | solution.py:67
  1766.1 13.4 collective-permute-done.1
  (329 shorter events, 370.4 us)
Async XLA Ops:
  7.2 41.8 %all-gather.2.cloned.1.call-start = ((), (), s32[]{:S(2)}) async-start(), calls=%async_computation | async-start | bytes 2228224 | tf_op jit(solution)/shard_map/all_gather | solution.py:38
  54.2 135.3 %all-reduce.2.cloned.1.call-start = ((), (), s32[]{:S(2)}) async-start(), calls=%async_computation.1 | async-start | bytes 1048576 | tf_op jit(solution)/shard_map/while/body/eval_jaxpr/psum | solution.py:67
  69.8 143.0 %collective-permute-start = (bf16[2,16,128,128]{2,3,0,1:T(8,128)(2,1)S(1)}, bf16[2,16,128,128]{2,3,0,1:T(8,128)(2,1)}, u32[]{:S(2)}, u32[]{:S(2)}) collective-permute-start(bf16[2,16,128,128]{2,3,0,1:T(8,128)(2,1)S(1)} %fusion.85), channel_id=1, source_target_pairs={{0,16},{16,32},{32,48},{48,64},{64,80},{80,96},{96,112},{1,17},{17... | collective-permute-start | bytes 3145736 | tf_op jit(solution)/shard_map/while/body/eval_jaxpr/ppermute | solution.py:10
  195.4 17.3 collective-permute-start.1
  212.7 133.3 %all-reduce.2.cloned.1.call-start = ((), (), s32[]{:S(2)}) async-start(), calls=%async_computation.1 | async-start | bytes 1048576 | tf_op jit(solution)/shard_map/while/body/eval_jaxpr/psum | solution.py:67
  228.3 141.1 %collective-permute-start = (bf16[2,16,128,128]{2,3,0,1:T(8,128)(2,1)S(1)}, bf16[2,16,128,128]{2,3,0,1:T(8,128)(2,1)}, u32[]{:S(2)}, u32[]{:S(2)}) collective-permute-start(bf16[2,16,128,128]{2,3,0,1:T(8,128)(2,1)S(1)} %fusion.85), channel_id=1, source_target_pairs={{0,16},{16,32},{32,48},{48,64},{64,80},{80,96},{96,112},{1,17},{17... | collective-permute-start | bytes 3145736 | tf_op jit(solution)/shard_map/while/body/eval_jaxpr/ppermute | solution.py:10
  369.3 133.4 %all-reduce.2.cloned.1.call-start = ((), (), s32[]{:S(2)}) async-start(), calls=%async_computation.1 | async-start | bytes 1048576 | tf_op jit(solution)/shard_map/while/body/eval_jaxpr/psum | solution.py:67
  384.9 141.1 %collective-permute-start = (bf16[2,16,128,128]{2,3,0,1:T(8,128)(2,1)S(1)}, bf16[2,16,128,128]{2,3,0,1:T(8,128)(2,1)}, u32[]{:S(2)}, u32[]{:S(2)}) collective-permute-start(bf16[2,16,128,128]{2,3,0,1:T(8,128)(2,1)S(1)} %fusion.85), channel_id=1, source_target_pairs={{0,16},{16,32},{32,48},{48,64},{64,80},{80,96},{96,112},{1,17},{17... | collective-permute-start | bytes 3145736 | tf_op jit(solution)/shard_map/while/body/eval_jaxpr/ppermute | solution.py:10
  526.0 133.4 %all-reduce.2.cloned.1.call-start = ((), (), s32[]{:S(2)}) async-start(), calls=%async_computation.1 | async-start | bytes 1048576 | tf_op jit(solution)/shard_map/while/body/eval_jaxpr/psum | solution.py:67
  541.6 141.1 %collective-permute-start = (bf16[2,16,128,128]{2,3,0,1:T(8,128)(2,1)S(1)}, bf16[2,16,128,128]{2,3,0,1:T(8,128)(2,1)}, u32[]{:S(2)}, u32[]{:S(2)}) collective-permute-start(bf16[2,16,128,128]{2,3,0,1:T(8,128)(2,1)S(1)} %fusion.85), channel_id=1, source_target_pairs={{0,16},{16,32},{32,48},{48,64},{64,80},{80,96},{96,112},{1,17},{17... | collective-permute-start | bytes 3145736 | tf_op jit(solution)/shard_map/while/body/eval_jaxpr/ppermute | solution.py:10
  682.7 133.4 %all-reduce.2.cloned.1.call-start = ((), (), s32[]{:S(2)}) async-start(), calls=%async_computation.1 | async-start | bytes 1048576 | tf_op jit(solution)/shard_map/while/body/eval_jaxpr/psum | solution.py:67
  698.2 141.1 %collective-permute-start = (bf16[2,16,128,128]{2,3,0,1:T(8,128)(2,1)S(1)}, bf16[2,16,128,128]{2,3,0,1:T(8,128)(2,1)}, u32[]{:S(2)}, u32[]{:S(2)}) collective-permute-start(bf16[2,16,128,128]{2,3,0,1:T(8,128)(2,1)S(1)} %fusion.85), channel_id=1, source_target_pairs={{0,16},{16,32},{32,48},{48,64},{64,80},{80,96},{96,112},{1,17},{17... | collective-permute-start | bytes 3145736 | tf_op jit(solution)/shard_map/while/body/eval_jaxpr/ppermute | solution.py:10
  839.3 133.4 %all-reduce.2.cloned.1.call-start = ((), (), s32[]{:S(2)}) async-start(), calls=%async_computation.1 | async-start | bytes 1048576 | tf_op jit(solution)/shard_map/while/body/eval_jaxpr/psum | solution.py:67
  854.9 141.1 %collective-permute-start = (bf16[2,16,128,128]{2,3,0,1:T(8,128)(2,1)S(1)}, bf16[2,16,128,128]{2,3,0,1:T(8,128)(2,1)}, u32[]{:S(2)}, u32[]{:S(2)}) collective-permute-start(bf16[2,16,128,128]{2,3,0,1:T(8,128)(2,1)S(1)} %fusion.85), channel_id=1, source_target_pairs={{0,16},{16,32},{32,48},{48,64},{64,80},{80,96},{96,112},{1,17},{17... | collective-permute-start | bytes 3145736 | tf_op jit(solution)/shard_map/while/body/eval_jaxpr/ppermute | solution.py:10
  996.0 133.4 %all-reduce.2.cloned.1.call-start = ((), (), s32[]{:S(2)}) async-start(), calls=%async_computation.1 | async-start | bytes 1048576 | tf_op jit(solution)/shard_map/while/body/eval_jaxpr/psum | solution.py:67
  1011.5 141.1 %collective-permute-start = (bf16[2,16,128,128]{2,3,0,1:T(8,128)(2,1)S(1)}, bf16[2,16,128,128]{2,3,0,1:T(8,128)(2,1)}, u32[]{:S(2)}, u32[]{:S(2)}) collective-permute-start(bf16[2,16,128,128]{2,3,0,1:T(8,128)(2,1)S(1)} %fusion.85), channel_id=1, source_target_pairs={{0,16},{16,32},{32,48},{48,64},{64,80},{80,96},{96,112},{1,17},{17... | collective-permute-start | bytes 3145736 | tf_op jit(solution)/shard_map/while/body/eval_jaxpr/ppermute | solution.py:10
  1152.6 133.4 %all-reduce.2.cloned.1.call-start = ((), (), s32[]{:S(2)}) async-start(), calls=%async_computation.1 | async-start | bytes 1048576 | tf_op jit(solution)/shard_map/while/body/eval_jaxpr/psum | solution.py:67
  1168.2 141.1 %collective-permute-start = (bf16[2,16,128,128]{2,3,0,1:T(8,128)(2,1)S(1)}, bf16[2,16,128,128]{2,3,0,1:T(8,128)(2,1)}, u32[]{:S(2)}, u32[]{:S(2)}) collective-permute-start(bf16[2,16,128,128]{2,3,0,1:T(8,128)(2,1)S(1)} %fusion.85), channel_id=1, source_target_pairs={{0,16},{16,32},{32,48},{48,64},{64,80},{80,96},{96,112},{1,17},{17... | collective-permute-start | bytes 3145736 | tf_op jit(solution)/shard_map/while/body/eval_jaxpr/ppermute | solution.py:10
  1309.3 133.5 %all-reduce.2.cloned.1.call-start = ((), (), s32[]{:S(2)}) async-start(), calls=%async_computation.1 | async-start | bytes 1048576 | tf_op jit(solution)/shard_map/while/body/eval_jaxpr/psum | solution.py:67
  1324.8 141.4 %collective-permute-start = (bf16[2,16,128,128]{2,3,0,1:T(8,128)(2,1)S(1)}, bf16[2,16,128,128]{2,3,0,1:T(8,128)(2,1)}, u32[]{:S(2)}, u32[]{:S(2)}) collective-permute-start(bf16[2,16,128,128]{2,3,0,1:T(8,128)(2,1)S(1)} %fusion.85), channel_id=1, source_target_pairs={{0,16},{16,32},{32,48},{48,64},{64,80},{80,96},{96,112},{1,17},{17... | collective-permute-start | bytes 3145736 | tf_op jit(solution)/shard_map/while/body/eval_jaxpr/ppermute | solution.py:10
  1466.2 133.4 %all-reduce.2.cloned.1.call-start = ((), (), s32[]{:S(2)}) async-start(), calls=%async_computation.1 | async-start | bytes 1048576 | tf_op jit(solution)/shard_map/while/body/eval_jaxpr/psum | solution.py:67
  1481.6 141.3 %collective-permute-start = (bf16[2,16,128,128]{2,3,0,1:T(8,128)(2,1)S(1)}, bf16[2,16,128,128]{2,3,0,1:T(8,128)(2,1)}, u32[]{:S(2)}, u32[]{:S(2)}) collective-permute-start(bf16[2,16,128,128]{2,3,0,1:T(8,128)(2,1)S(1)} %fusion.85), channel_id=1, source_target_pairs={{0,16},{16,32},{32,48},{48,64},{64,80},{80,96},{96,112},{1,17},{17... | collective-permute-start | bytes 3145736 | tf_op jit(solution)/shard_map/while/body/eval_jaxpr/ppermute | solution.py:10
  1622.9 133.4 %all-reduce.2.cloned.1.call-start = ((), (), s32[]{:S(2)}) async-start(), calls=%async_computation.1 | async-start | bytes 1048576 | tf_op jit(solution)/shard_map/while/body/eval_jaxpr/psum | solution.py:67
  1638.4 141.1 %collective-permute-start = (bf16[2,16,128,128]{2,3,0,1:T(8,128)(2,1)S(1)}, bf16[2,16,128,128]{2,3,0,1:T(8,128)(2,1)}, u32[]{:S(2)}, u32[]{:S(2)}) collective-permute-start(bf16[2,16,128,128]{2,3,0,1:T(8,128)(2,1)S(1)} %fusion.85), channel_id=1, source_target_pairs={{0,16},{16,32},{32,48},{48,64},{64,80},{80,96},{96,112},{1,17},{17... | collective-permute-start | bytes 3145736 | tf_op jit(solution)/shard_map/while/body/eval_jaxpr/ppermute | solution.py:10
  (16 other events, 277.9 us)
Sparse Core Ops, SparseCore 0:
  9.6 39.2 all-gather.1
  69.9 119.5 all-reduce.1
  228.4 117.6 all-reduce.1
  385.0 117.6 all-reduce.1
  541.7 117.6 all-reduce.1
  698.3 117.6 all-reduce.1
  855.0 117.6 all-reduce.1
  1011.6 117.6 all-reduce.1
  1168.3 117.6 all-reduce.1
  1324.9 117.8 all-reduce.1
  1481.7 117.7 all-reduce.1
  1638.6 117.6 all-reduce.1
where the time goes:
time: 1790 us
  waiting for transfers between devices  1400 us (78%)
  local copies, waits for them, and re-layouts  147 us (8%)
  matrix products  145 us (8%)
  other arithmetic  49.4 us (3%)
  starting transfers between devices  28.4 us (2%)
    psum x11, waiting for transfers between devices, section(): lax.psum(partial_value.astype(jnp.bfloat16), 'op').astype(jnp.float32)  1220 us
    ppermute x22, waiting for transfers between devices, shifted(): return lax.ppermute(x, axis, pairs)  147 us
    dot_general x11, matrix products, advance_terms(): jnp.einsum('srab,ksrac->krbc', amat, scaled, preferred_element_type=jnp.f...  66 us
    dot_general x11, matrix products, carry_block(): jnp.einsum('srab,srac->rbc', bra_rows, moved, preferred_element_type=jnp....  65.5 us
  transfers between devices with their start and end apart: 34, of which 23 were waited for; matrix products, arithmetic and copies ran while one was open for 9% of the time, Pallas kernels for 0%

commit v1 on v0

v1 whole, which is shorter than its diff:
```python
import functools

import jax
import jax.numpy as jnp
from jax import lax
from jax.experimental import pallas as pl
from jax.experimental.pallas import tpu as pltpu
from jax.sharding import PartitionSpec as P

MESH = pl.DeviceIdType.MESH
F32 = jnp.float32
BF16 = jnp.bfloat16
SITES, ROOTS, STATES, SECTORS, B = 8, 4, 4, 16, 128
CHAINS = 3
UNROLL = 4


class Place:
    def __init__(self):
        site = lax.axis_index("site")
        op = lax.axis_index("op")
        self.site, self.op = site, op
        self.h, self.y = lax.rem(site, 2), site // 2
        self.l, self.z, self.c = op // 8, lax.rem(op // 2, 4), lax.rem(op, 2)
        self.x = 2 * self.h + self.l

    def along_x(self, by):
        x = lax.rem(self.x + by, 4)
        return {"site": 2 * self.y + x // 2, "op": 8 * lax.rem(x, 2) + 2 * self.z + self.c}

    def along_z(self, by):
        z = lax.rem(self.z + by, 4)
        return {"site": self.site, "op": 8 * self.l + 2 * z + self.c}

    def along_y(self, by):
        return {"site": 2 * lax.rem(self.y + by, 4) + self.h, "op": self.op}

    def row(self, y):
        return {"site": 2 * y + self.h, "op": self.op}

    def sibling(self):
        return {"site": self.site, "op": self.op + 1 - 2 * self.c}

    def along_site(self, by):
        return {"site": lax.rem(self.site + by, SITES), "op": self.op}

    def group(self, g):
        return {"site": self.site, "op": 2 * g + self.c}


def kernel(ints_ref, floats_ref, rows_ref, mps_ref, env_ref, out_terms, out_block, *scratch):
    scratch = list(scratch)
    a_bufs = [scratch.pop(0) for _ in range(SITES)]
    x_bufs = [scratch.pop(0) for _ in range(SITES + 1)]
    h_bufs = [scratch.pop(0) for _ in range(SITES)]
    (s_buf, core_buf, part_buf, ring_buf, final_buf, ints_all, floats_all, ints, floats,
     param_s, param_r, param_l, y_s, y_r, xa_s, xa_r, za_s, za_r, xb_s, xb_r, zb_s, zb_r, c_s, c_r,
     env_l, out_s, out_r, h1_s, h1_r, h2_s, h2_r, h3_s, h3_r) = scratch
    me = Place()

    def remote(src, dst, send, recv, device):
        return pltpu.make_async_remote_copy(
            src_ref=src, dst_ref=dst, send_sem=send, recv_sem=recv, device_id=device, device_id_type=MESH
        )

    def arrival(dst, recv):
        pltpu.make_async_copy(dst, dst, recv).wait()

    barrier = pltpu.get_barrier_semaphore()
    partners = [me.along_site(d) for d in range(1, SITES)]
    partners += [me.along_x(1), me.along_x(3)]
    partners += [me.along_z(d) for d in (1, 2, 3)]
    partners += [me.sibling()]
    g_me = me.op // 2
    partners += [
        {"site": me.site, "op": 8 * (1 - me.l) + 2 * lax.rem(me.z + d, 4) + me.c} for d in (1, 2, 3)
    ]
    for device in partners:
        pl.semaphore_signal(barrier, inc=1, device_id=device, device_id_type=MESH)
    pl.semaphore_wait(barrier, len(partners))

    sends = []

    def start(copy):
        copy.start()
        sends.append(copy)

    for d in range(1, SITES):
        start(remote(ints_ref, ints_all.at[me.site], param_s.at[0, d], param_r.at[0, me.site], me.along_site(d)))
        start(remote(floats_ref, floats_all.at[me.site], param_s.at[1, d], param_r.at[1, me.site], me.along_site(d)))

    def piece(q):
        return mps_ref.at[q, :, me.op]

    def slot(i):
        return a_bufs[i].at[me.l, me.z, me.c]

    def own(i):
        return me.h == i % 2

    for i in range(SITES):
        @pl.when(me.site == i)
        def _():
            for d in (1, 2, 3):
                q = lax.rem(me.y + d, 4)
                remote(piece(q), slot(i), y_s.at[d], y_r.at[i // 2], me.along_y(d)).start()
            pltpu.make_async_copy(piece(me.y), slot(i), y_r.at[i // 2]).start()

    env_copies = []
    for k in range(2):
        copy = pltpu.make_async_copy(env_ref.at[me.y, k], x_bufs[0].at[:, k], env_l.at[k])
        copy.start()
        env_copies.append(copy)

    row_group = lax.broadcasted_iota(jnp.int32, (B, B), 0) // 8
    def init(e, _):
        tiled = jnp.concatenate([rows_ref[e]] * (B // 8), axis=0)
        x_bufs[0][e, 2] = jnp.where(row_group == me.op, tiled, 0.0).astype(BF16)
        return 0
    lax.fori_loop(0, SECTORS, init, 0)

    first, second = pl.ds(0, 2), pl.ds(2, 2)

    def p1(i):
        @pl.when(own(i))
        def _():
            arrival(slot(i), y_r.at[i // 2])
            a = a_bufs[i]
            for d in (1, 3, 2):
                part = a.at[me.l, me.z, me.c, first]
                remote(part, part, xa_s.at[i, d - 1], xa_r.at[i, me.l], me.along_x(d)).start()
                part = a.at[me.l, me.z, me.c, second]
                remote(part, part, za_s.at[i, d - 1], za_r.at[i, me.z], me.along_z(d)).start()

    def p2(i):
        a = a_bufs[i]
        for l in range(2):
            @pl.when(jnp.logical_not(jnp.logical_and(own(i), me.l == l)))
            def _():
                arrival(a.at[l, me.z, me.c, first], xa_r.at[i, l])
        for d in (1, 3, 2):
            part = a.at[:, me.z, me.c, first]
            start(remote(part, part, zb_s.at[i, d - 1], zb_r.at[i, me.z], me.along_z(d)))

        @pl.when(own(i))
        def _():
            for d in (1, 3, 2):
                z = lax.rem(me.z + d, 4)
                arrival(a.at[me.l, z, me.c, second], za_r.at[i, z])
            for d in (1, 3, 2):
                part = a.at[me.l, :, me.c, second]
                remote(part, part, xb_s.at[i, d - 1], xb_r.at[i, me.l], me.along_x(d)).start()

    def p3(i):
        a = a_bufs[i]
        for d in (1, 3, 2):
            z = lax.rem(me.z + d, 4)
            arrival(a.at[:, z, me.c, first], zb_r.at[i, z])
        for l in range(2):
            @pl.when(jnp.logical_not(jnp.logical_and(own(i), me.l == l)))
            def _():
                arrival(a.at[l, :, me.c, second], xb_r.at[i, l])
        part = a.at[:, :, me.c]
        start(remote(part, part, c_s.at[i], c_r.at[i], me.sibling()))

    def p4(i):
        arrival(a_bufs[i].at[:, :, 1 - me.c], c_r.at[i])

    column = lax.broadcasted_iota(jnp.int32, (1, B), 1)
    row = lax.broadcasted_iota(jnp.int32, (B, 1), 0)

    def multiply(i):
        a, x, new, h = a_bufs[i], x_bufs[i], x_bufs[i + 1], h_bufs[i]

        def first_product(e, _):
            wide, scale = [], []
            for s in range(STATES):
                r = ints[i, 0, 64 + s * SECTORS + e]
                wide.append(a[r // 8, lax.rem(r // 2, 4), lax.rem(r, 2), s])
                live = column < ints[i, 1, r]
                scale.append(
                    [jnp.where(live, floats[i, 0, k * STATES + s], 0.0) for k in range(2)]
                    + [jnp.where(live, 1.0, 0.0)]
                )
            product = jnp.dot(
                x[e].reshape(CHAINS * B, B), jnp.concatenate(wide, axis=1), preferred_element_type=F32
            )
            for s in range(STATES):
                s_buf[e, s] = jnp.concatenate(
                    [
                        (product[k * B : (k + 1) * B, s * B : (s + 1) * B] * scale[s][k]).astype(BF16)
                        for k in range(CHAINS)
                    ],
                    axis=1,
                )
            return 0

        lax.fori_loop(0, SECTORS, first_product, 0, unroll=UNROLL)

        def second_product(pair, _):
            blocks = []
            for part in range(2):
                r = 2 * pair + part
                scaled = jnp.concatenate([s_buf[ints[i, 0, s * SECTORS + r], s] for s in range(STATES)], axis=0)
                tensor = a[pair // 4, lax.rem(pair, 4), part].reshape(STATES * B, B)
                mixed = lax.dot_general(
                    tensor, scaled, (((0,), (0,)), ((), ())), preferred_element_type=F32
                )
                mixed = jnp.where(row < ints[i, 1, r], mixed, 0.0)
                chains = [mixed[:, k * B : (k + 1) * B] for k in range(CHAINS)]
                chains[2] = chains[2] + floats[i, 0, 8] * chains[0] + floats[i, 0, 9] * chains[1]
                for k in range(CHAINS):
                    new[r, k] = chains[k].astype(BF16)
                blocks.append(chains[2].reshape(SECTORS, 8, B))
            h[:, :, pair] = jnp.concatenate(blocks, axis=1).astype(BF16).reshape(8, 2, 16, B)
            return 0

        lax.fori_loop(0, SECTORS // 2, second_product, 0, unroll=UNROLL // 2)

    def out(i):
        target = i // 2

        @pl.when(own(i))
        def _():
            for k in range(2):
                src, dst = x_bufs[i + 1].at[:, k], out_terms.at[me.y, k]

                @pl.when(me.y == target)
                def _():
                    pltpu.make_async_copy(src, dst, out_r.at[me.y, k]).start()

                @pl.when(me.y != target)
                def _():
                    remote(src, dst, out_s.at[target, k], out_r.at[me.y, k], me.row(target)).start()

    def h1(i):
        @pl.when(own(i))
        def _():
            remote(h_bufs[i].at[:, 1 - me.c], core_buf.at[i // 2], h1_s.at[i // 2], h1_r.at[i // 2], me.sibling()).start()

    def h2(i):
        n = i // 2

        @pl.when(own(i))
        def _():
            arrival(core_buf.at[n], h1_r.at[n])
            for g in range(8):
                part_buf[n, g] = (
                    h_bufs[i][g, me.c].astype(F32) + core_buf[n, g].astype(F32)
                ).astype(BF16)
            for g in range(8):
                @pl.when(g_me != g)
                def _():
                    remote(part_buf.at[n, g], ring_buf.at[n, g_me], h2_s.at[n, g], h2_r.at[n, g_me], me.group(g)).start()

    def h3(i):
        n = i // 2

        @pl.when(own(i))
        def _():
            total = part_buf[n, g_me].astype(F32)
            for d in range(1, 8):
                g = lax.rem(g_me + d, 8)
                arrival(ring_buf.at[n, g], h2_r.at[n, g])
                total = total + ring_buf[n, g].astype(F32)
            final_buf[n] = total.astype(BF16)

            @pl.when(me.y == n)
            def _():
                pltpu.make_async_copy(final_buf.at[n], out_block.at[me.y], h3_r.at[me.y]).start()

            @pl.when(me.y != n)
            def _():
                remote(final_buf.at[n], out_block.at[me.y], h3_s.at[n], h3_r.at[me.y], me.row(n)).start()

    p1(0)
    ints_all[me.site] = ints_ref[...]
    floats_all[me.site] = floats_ref[...]
    for d in range(1, SITES):
        site = lax.rem(me.site + d, SITES)
        arrival(ints_all.at[site], param_r.at[0, site])
        arrival(floats_all.at[site], param_r.at[1, site])
    to_smem = [
        pltpu.make_async_copy(ints_all, ints, param_l.at[0]),
        pltpu.make_async_copy(floats_all, floats, param_l.at[1]),
    ]
    for copy in to_smem:
        copy.start()
    p1(1)
    p2(0)
    for copy in to_smem + env_copies:
        copy.wait()
    p1(2)
    p2(1)
    p3(0)
    for i in range(SITES + 2):
        if i + 3 < SITES:
            p1(i + 3)
        if i + 2 < SITES:
            p2(i + 2)
        if i + 1 < SITES:
            p3(i + 1)
        if 0 <= i - 1 < SITES:
            h2(i - 1)
        if 0 <= i - 2 < SITES:
            h3(i - 2)
        if i < SITES:
            p4(i)
            multiply(i)
            out(i)
            h1(i)

    for q in range(ROOTS):
        for k in range(2):
            arrival(out_terms.at[q, k], out_r.at[q, k])
        arrival(out_block.at[q], h3_r.at[q])
    for copy in sends:
        copy.wait_send()

    def left(src, sem):
        pltpu.make_async_copy(src, src, sem).wait()

    for d in (1, 2, 3):
        left(piece(0), y_s.at[d])
    for i in range(SITES):
        @pl.when(own(i))
        def _():
            for d in (1, 2, 3):
                left(a_bufs[i].at[0, 0, 0, first], xa_s.at[i, d - 1])
                left(a_bufs[i].at[0, 0, 0, first], za_s.at[i, d - 1])
                left(a_bufs[i].at[0, :, 0, first], xb_s.at[i, d - 1])
            left(core_buf.at[i // 2], h1_s.at[i // 2])
            for g in range(8):
                @pl.when(g_me != g)
                def _():
                    left(part_buf.at[i // 2, g], h2_s.at[i // 2, g])

            @pl.when(me.y != i // 2)
            def _():
                for k in range(2):
                    left(x_bufs[i + 1].at[:, k], out_s.at[i // 2, k])
                left(final_buf.at[i // 2], h3_s.at[i // 2])


def shards(mps, sector_map, live_rows, term_mask, term_coef, block_coef, env_terms, env_block):
    row = lax.axis_index("site") // 2
    source = sector_map[0]
    inverse = jnp.sum(
        jnp.where(source[:, None, :] == jnp.arange(SECTORS)[None, :, None], jnp.arange(SECTORS)[None, None, :], 0),
        axis=2,
    ).astype(jnp.int32)
    ints = jnp.concatenate([source.reshape(-1), inverse.reshape(-1), live_rows[0], jnp.zeros((880,), jnp.int32)])
    weights = term_coef[0] * term_mask[0].astype(F32)
    floats = jnp.concatenate([weights.reshape(-1), block_coef[0], jnp.zeros((1014,), F32)])
    rows = lax.dynamic_index_in_dim(env_block, row, 0, False).astype(F32)
    dma = pltpu.SemaphoreType.DMA
    vmem = pltpu.VMEM
    scratch = [vmem((2, 4, 2, STATES, B, B), BF16)] * SITES
    scratch += [vmem((SECTORS, CHAINS, B, B), BF16)] * (SITES + 1)
    scratch += [vmem((8, 2, 8, 16, B), BF16)] * SITES
    scratch += [
        vmem((SECTORS, STATES, B, CHAINS * B), BF16),
        vmem((4, 8, 8, 16, B), BF16),
        vmem((4, 8, 8, 16, B), BF16),
        vmem((4, 8, 8, 16, B), BF16),
        vmem((4, 8, 16, B), BF16),
        vmem((SITES, 8, B), jnp.int32),
        vmem((SITES, 8, B), F32),
        pltpu.SMEM((SITES, 8, B), jnp.int32),
        pltpu.SMEM((SITES, 8, B), F32),
        dma((2, SITES)), dma((2, SITES)), dma((2,)),
        dma((4,)), dma((4,)),
        dma((SITES, 3)), dma((SITES, 2)),
        dma((SITES, 3)), dma((SITES, 4)),
        dma((SITES, 3)), dma((SITES, 2)),
        dma((SITES, 3)), dma((SITES, 4)),
        dma((SITES,)), dma((SITES,)),
        dma((2,)),
        dma((4, 2)), dma((4, 2)),
        dma((4,)), dma((4,)),
        dma((4, 8)), dma((4, 8)),
        dma((4,)), dma((4,)),
    ]
    anywhere = pl.BlockSpec(memory_space=pl.ANY)
    inside = pl.BlockSpec(memory_space=pltpu.VMEM)
    terms, block = pl.pallas_call(
        kernel,
        out_shape=(
            jax.ShapeDtypeStruct((ROOTS, 2, SECTORS, B, B), BF16),
            jax.ShapeDtypeStruct((ROOTS, 8, 16, B), BF16),
        ),
        in_specs=[inside, inside, inside, anywhere, anywhere],
        out_specs=(anywhere, anywhere),
        scratch_shapes=scratch,
        compiler_params=pltpu.CompilerParams(
            collective_id=0, has_side_effects=True, vmem_limit_bytes=56 * 2**20
        ),
        name="chains",
    )(ints.reshape(8, B), floats.reshape(8, B), rows, mps[0], env_terms)
    return terms[None], block.reshape(1, ROOTS, SECTORS, 8, B)


def solution(mesh):
    in_specs = (
        P("site", None, None, None, None, None),
        P("site", None, None),
        P("site", None),
        P("site", "op", None),
        P("site", "op", None),
        P("site", "op"),
        P(None, "op", None, None, None),
        P(None, None, "op", None),
    )
    out_specs = (P("site", None, "op", None, None, None), P("site", None, None, "op", None))
    return jax.shard_map(shards, mesh=mesh, in_specs=in_specs, out_specs=out_specs, check_vma=False)
```

time: 1790 us -> 156 us (0.09)
  waiting for transfers between devices: 1400 us -> 0 us
  matrix products: 145 us -> 0 us
  Pallas kernels: 0 us -> 142 us
  local copies, waits for them, and re-layouts: 147 us -> 6.42 us
  other arithmetic: 49.4 us -> 5.57 us
  starting transfers between devices: 28.4 us -> 0 us
    psum x11 -> x0, waiting for transfers between devices: 1220 us -> none  [section(): lax.psum(partial_value.astype(jnp.bfloat16), 'op').astype(jnp.float32)]
    ppermute x22 -> x0, waiting for transfers between devices: 147 us -> none  [shifted(): return lax.ppermute(x, axis, pairs)]
    dot_general x33 -> x0, matrix products: 145 us -> none  [the longest x11 66 us: advance_terms(): jnp.einsum('srab,ksrac->krbc', amat, scaled, preferred_element_type=jnp.f...]
    pallas_call x0 -> x1, Pallas kernels: none -> 142 us  [shards(): pl.pallas_call(kernel, out_shape=(jax.ShapeDtypeStruct((ROOTS, 2, SECTORS...]
    gather x22 -> x0, local copies, waits for them, and re-layouts: 57.5 us -> none  [the longest x11 33.5 us: advance_terms(): source = jnp.take(terms, sector_rows, axis=1)]
    dynamic_slice x55 -> x0, local copies, waits for them, and re-layouts: 43.3 us -> none  [the longest x22 21.6 us: section(): old_terms = lax.dynamic_index_in_dim(out_terms, slot, 0, False)]
    all_gather x1 -> x0, waiting for transfers between devices: 29.5 us -> none  [shards(): start_block = lax.all_gather(env_block, 'op', axis=2, tiled=True)]
    select_n x33 -> x0, other arithmetic: 28.7 us -> none  [the longest x11 14.7 us: section(): jnp.where(place == 0, lax.dynamic_index_in_dim(env_terms, first, 0, False...]
  transfers between devices with their start and end apart: 34 -> 0, of which waited for: 23 -> 0; matrix products, arithmetic and copies ran while one was open for 9% -> 0% of each run, Pallas kernels for 0% -> 0%
where the time goes in v1:
time: 156 us; the launch traced here: 155 us
  Pallas kernels  142 us (91%)
  local copies, waits for them, and re-layouts  6.42 us (4%)
  other arithmetic  5.57 us (4%)
    pallas_call x1, Pallas kernels, shards(): pl.pallas_call(kernel, out_shape=(jax.ShapeDtypeStruct((ROOTS, 2, SECTORS...  142 us
    unnamed x4, local copies, waits for them, and re-layouts  5.48 us

profile of v1, /device:TPU:28, one launch (start us, length us, event | category | flops | bytes accessed | tf_op | source)
XLA Modules:
  0.0 155.1 jit_solution(15812604899723001081)
XLA Ops:
  0.6 0.8 reshape_squeeze.3
  1.4 0.7 convert_multiply_fusion
  2.1 0.1 mul.8
  2.2 0.8 select_reduce_fusion
  3.0 0.1 reshape.24
  3.1 1.3 add_bitcast_fusion.ints_ref
  4.4 1.3 maximum_bitcast_fusion.floats_ref
  5.8 1.4 bitcast_convert_fusion.rows_ref
  7.2 142.5 %chains.1 = (bf16[4,2,16,128,128]{4,3,2,1,0:T(8,128)(2,1)}, bf16[4,8,16,128]{3,2,1,0:T(8,128)(2,1)}) custom-call(s32[8,128]{1,0:T(8,128)} %add_bitcast_fusion.ints_ref, f32[8,128]{1,0:T(8,128)} %maximum_bitcast_fusion.floats_ref, f32[16,8,128]{2,1,0:T(8,128)} %bitcast_convert_fusion.rows_ref, bf16[4,4,16,128,128]{4,3,2,1,0:T(8,128)(2,1)} %bitcast.13, ...), custom_call_target="tpu_custom_call" | custom-call | tf_op jit(solution)/shard_map/chains/pallas_call | solution.py:386
  149.6 0.0 copy-start
  149.7 4.8 %copy.12 = bf16[1,4,2,16,128,128]{5,4,3,2,1,0:T(8,128)(2,1)} copy(bf16[1,4,2,16,128,128]{5,4,3,2,1,0:T(8,128)(2,1)} %bitcast.14) | data formatting | bytes 8388608
  154.5 0.0 copy-done
  154.5 0.7 copy.13
  (2 shorter events, 0.0 us)
Async XLA Ops:
  149.6 4.8 %copy-start = (bf16[4,8,16,128]{3,2,1,0:T(8,128)(2,1)S(1)}, bf16[4,8,16,128]{3,2,1,0:T(8,128)(2,1)}, u32[]{:S(2)}) copy-start(bf16[4,8,16,128]{3,2,1,0:T(8,128)(2,1)} %get-tuple-element.5) | copy-start | bytes 393220

commit v2 on v1

v2 whole, which is shorter than its diff:
```python
import functools

import jax
import jax.numpy as jnp
from jax import lax
from jax.experimental import pallas as pl
from jax.experimental.pallas import tpu as pltpu
from jax.sharding import PartitionSpec as P

MESH = pl.DeviceIdType.MESH
F32 = jnp.float32
BF16 = jnp.bfloat16
SITES, ROOTS, STATES, SECTORS, B = 8, 4, 4, 16, 128
CHAINS = 3
UNROLL = 8
EARLY = 2


class Place:
    def __init__(self):
        site = lax.axis_index("site")
        op = lax.axis_index("op")
        self.site, self.op = site, op
        self.h, self.y = lax.rem(site, 2), site // 2
        self.l, self.z, self.c = op // 8, lax.rem(op // 2, 4), lax.rem(op, 2)
        self.x = 2 * self.h + self.l

    def along_x(self, by):
        x = lax.rem(self.x + by, 4)
        return {"site": 2 * self.y + x // 2, "op": 8 * lax.rem(x, 2) + 2 * self.z + self.c}

    def along_z(self, by):
        z = lax.rem(self.z + by, 4)
        return {"site": self.site, "op": 8 * self.l + 2 * z + self.c}

    def along_y(self, by):
        return {"site": 2 * lax.rem(self.y + by, 4) + self.h, "op": self.op}

    def row(self, y):
        return {"site": 2 * y + self.h, "op": self.op}

    def sibling(self):
        return {"site": self.site, "op": self.op + 1 - 2 * self.c}

    def along_site(self, by):
        return {"site": lax.rem(self.site + by, SITES), "op": self.op}

    def group(self, g):
        return {"site": self.site, "op": 2 * g + self.c}


def kernel(map_ref, live_ref, mask_ref, coef_ref, pair_ref, block_ref, mps_ref, env_ref, out_terms, out_block, *scratch):
    scratch = list(scratch)
    a_bufs = [scratch.pop(0) for _ in range(SITES)]
    x_bufs = [scratch.pop(0) for _ in range(SITES + 1)]
    h_bufs = [scratch.pop(0) for _ in range(SITES)]
    (s_buf, core_buf, part_buf, ring_buf, final_buf, ints_all, floats_all, ints, floats,
     rows_buf, relay_buf, param_s, param_r, param_l, ya_s, ya_r, yb_s, yb_r, xa_s, xa_r, za_s, za_r, xb_s, xb_r, zb_s, zb_r, c_s, c_r,
     env_l, out_s, out_r, relay_s, relay_r, h1_s, h1_r, h2_s, h2_r, h3_s, h3_r) = scratch
    me = Place()

    def remote(src, dst, send, recv, device):
        return pltpu.make_async_remote_copy(
            src_ref=src, dst_ref=dst, send_sem=send, recv_sem=recv, device_id=device, device_id_type=MESH
        )

    def arrival(dst, recv):
        pltpu.make_async_copy(dst, dst, recv).wait()

    env_copies = [pltpu.make_async_copy(block_ref.at[me.y], rows_buf, env_l.at[2])]
    for k in range(2):
        env_copies.append(pltpu.make_async_copy(env_ref.at[me.y, k], x_bufs[0].at[:, k], env_l.at[k]))
    for copy in env_copies:
        copy.start()

    source = lax.broadcasted_iota(jnp.int32, (SECTORS, SECTORS), 0)
    target = lax.broadcasted_iota(jnp.int32, (SECTORS, SECTORS), 1)
    lane = lax.broadcasted_iota(jnp.int32, (SECTORS, B), 1)
    inverse = jnp.zeros((SECTORS, B), jnp.int32)
    for s in range(STATES):
        found = jnp.max(jnp.where(map_ref[pl.ds(s, 1), :] == source, target, 0), axis=1, keepdims=True)
        inverse = jnp.where(lane == s, found, inverse)
    ints_all[me.site] = jnp.zeros((24, B), jnp.int32)
    ints_all[me.site, pl.ds(0, STATES), pl.ds(0, SECTORS)] = map_ref[...]
    ints_all[me.site, pl.ds(4, 1), pl.ds(0, SECTORS)] = live_ref[...]
    ints_all[me.site, pl.ds(8, SECTORS), :] = inverse
    floats_all[me.site] = jnp.zeros((8, B), F32)
    floats_all[me.site, pl.ds(0, 2), pl.ds(0, STATES)] = coef_ref[...] * mask_ref[...].astype(F32)
    floats_all[me.site, pl.ds(2, 1), pl.ds(0, 2)] = pair_ref[...]

    barrier = pltpu.get_barrier_semaphore()
    partners = [me.along_site(d) for d in range(1, SITES)]
    partners += [me.along_x(1), me.along_x(3)]
    partners += [me.along_z(d) for d in (1, 2, 3)]
    partners += [me.sibling()]
    g_me = me.op // 2
    partners += [
        {"site": me.site, "op": 8 * (1 - me.l) + 2 * lax.rem(me.z + d, 4) + me.c} for d in (1, 2, 3)
    ]
    for device in partners:
        pl.semaphore_signal(barrier, inc=1, device_id=device, device_id_type=MESH)
    pl.semaphore_wait(barrier, len(partners))

    sends = []

    def start(copy):
        copy.start()
        sends.append(copy)

    for d in range(1, SITES):
        start(remote(ints_all.at[me.site], ints_all.at[me.site], param_s.at[0, d], param_r.at[0, me.site], me.along_site(d)))
        start(remote(floats_all.at[me.site], floats_all.at[me.site], param_s.at[1, d], param_r.at[1, me.site], me.along_site(d)))

    first, second = pl.ds(0, 2), pl.ds(2, 2)

    def own(i):
        return me.h == i % 2

    def first_parts(q, i):
        return [(mps_ref.at[q, first, me.l, me.z, me.c], a_bufs[i].at[me.l, me.z, me.c, first], 0)]

    def second_parts(q, i):
        if i < EARLY:
            return [(mps_ref.at[q, second, me.l, me.z, me.c], a_bufs[i].at[me.l, me.z, me.c, second], 0)]
        return [(mps_ref.at[q, 2 + n, me.l, :, me.c], a_bufs[i].at[me.l, :, me.c, 2 + n], n) for n in range(2)]

    def spread(parts, send, recv, sites):
        for i in sites:
            @pl.when(me.site == i)
            def _():
                for d in (2, 1, 3):
                    for src, dst, n in parts(lax.rem(me.y + d, 4), i):
                        remote(src, dst, send.at[d, n], recv.at[i // 2, n], me.along_y(d)).start()
                for src, dst, n in parts(me.y, i):
                    pltpu.make_async_copy(src, dst, recv.at[i // 2, n]).start()

    spread(first_parts, ya_s, ya_r, range(SITES))
    spread(second_parts, yb_s, yb_r, range(SITES))

    row_group = lax.broadcasted_iota(jnp.int32, (B, B), 0) // 8
    env_copies[0].wait()

    def init(pair, _):
        both = rows_buf[pair].astype(F32)
        for part in range(2):
            tiled = jnp.concatenate([both[8 * part : 8 * part + 8]] * (B // 8), axis=0)
            x_bufs[0][2 * pair + part, 2] = jnp.where(row_group == me.op, tiled, 0.0).astype(BF16)
        return 0

    lax.fori_loop(0, SECTORS // 2, init, 0)


    beside = me.along_x(1 + 2 * me.l)
    across = me.along_x(3 - 2 * me.l)
    last = SITES - 1

    def wanted(i):
        return own(i) if i == last else me.h >= 0

    def send_second(i):
        part = a_bufs[i].at[me.l, :, me.c, second]
        for n, device in enumerate([beside] if i == last else [across, beside, me.along_x(2)]):
            remote(part, part, xb_s.at[i, n], xb_r.at[i, me.l], device).start()

    def p1(i):
        a = a_bufs[i]

        @pl.when(own(i))
        def _():
            part = a.at[me.l, me.z, me.c, first]
            arrival(part, ya_r.at[i // 2, 0])
            targets = [beside] if i == last else [across, beside, me.along_x(2)]
            for n, device in enumerate(targets):
                remote(part, part, xa_s.at[i, n], xa_r.at[i, me.l], device).start()
            if i < EARLY:
                part = a.at[me.l, me.z, me.c, second]
                arrival(part, yb_r.at[i // 2, 0])
                for d in (1, 3, 2):
                    remote(part, part, za_s.at[i, d - 1], za_r.at[i, me.z], me.along_z(d)).start()

    def p2(i):
        a = a_bufs[i]

        @pl.when(own(i))
        def _():
            if i < EARLY:
                for d in (1, 3, 2):
                    z = lax.rem(me.z + d, 4)
                    arrival(a.at[me.l, z, me.c, second], za_r.at[i, z])
            else:
                for n in range(2):
                    arrival(a.at[me.l, :, me.c, 2 + n], yb_r.at[i // 2, n])
            send_second(i)

        @pl.when(wanted(i))
        def _():
            for l in range(2):
                @pl.when(jnp.logical_not(jnp.logical_and(own(i), me.l == l)))
                def _():
                    arrival(a.at[l, me.z, me.c, first], xa_r.at[i, l])
            for d in (1, 3, 2):
                part = a.at[:, me.z, me.c, first]
                remote(part, part, zb_s.at[i, d - 1], zb_r.at[i, me.z], me.along_z(d)).start()

    def p3(i):
        a = a_bufs[i]

        @pl.when(wanted(i))
        def _():
            for d in (1, 3, 2):
                z = lax.rem(me.z + d, 4)
                arrival(a.at[:, z, me.c, first], zb_r.at[i, z])

            @pl.when(own(i))
            def _():
                arrival(a.at[1 - me.l, :, me.c, second], xb_r.at[i, 1 - me.l])

            @pl.when(jnp.logical_not(own(i)))
            def _():
                for l in range(2):
                    arrival(a.at[l, :, me.c, second], xb_r.at[i, l])
            part = a.at[:, :, me.c]
            remote(part, part, c_s.at[i], c_r.at[i], me.sibling()).start()

    def p4(i):
        @pl.when(wanted(i))
        def _():
            arrival(a_bufs[i].at[:, :, 1 - me.c], c_r.at[i])

    column = lax.broadcasted_iota(jnp.int32, (1, B), 1)
    row = lax.broadcasted_iota(jnp.int32, (B, 1), 0)

    def multiply_first(i):
        a, x = a_bufs[i], x_bufs[i]

        def first_product(e, _):
            wide, scale = [], []
            for s in range(STATES):
                r = ints[i, 8 + e, s]
                wide.append(a[r // 8, lax.rem(r // 2, 4), lax.rem(r, 2), s])
                live = column < ints[i, 4, r]
                scale.append(
                    [jnp.where(live, floats[i, k, s], 0.0) for k in range(2)]
                    + [jnp.where(live, 1.0, 0.0)]
                )
            product = jnp.dot(
                x[e].reshape(CHAINS * B, B), jnp.concatenate(wide, axis=1), preferred_element_type=F32
            )
            for s in range(STATES):
                s_buf[e, s] = jnp.concatenate(
                    [
                        (product[k * B : (k + 1) * B, s * B : (s + 1) * B] * scale[s][k]).astype(BF16)
                        for k in range(CHAINS)
                    ],
                    axis=1,
                )
            return 0

        lax.fori_loop(0, SECTORS, first_product, 0, unroll=UNROLL)

    def multiply_second(i):
        a, new, h = a_bufs[i], x_bufs[i + 1], h_bufs[i]

        def second_product(pair, _):
            blocks = []
            for part in range(2):
                r = 2 * pair + part
                scaled = jnp.concatenate([s_buf[ints[i, s, r], s] for s in range(STATES)], axis=0)
                tensor = a[pair // 4, lax.rem(pair, 4), part].reshape(STATES * B, B)
                mixed = lax.dot_general(
                    tensor, scaled, (((0,), (0,)), ((), ())), preferred_element_type=F32
                )
                mixed = jnp.where(row < ints[i, 4, r], mixed, 0.0)
                chains = [mixed[:, k * B : (k + 1) * B] for k in range(CHAINS)]
                chains[2] = chains[2] + floats[i, 2, 0] * chains[0] + floats[i, 2, 1] * chains[1]
                for k in range(CHAINS):
                    new[r, k] = chains[k].astype(BF16)
                blocks.append(chains[2].reshape(SECTORS, 8, B))
            h[:, :, pair] = jnp.concatenate(blocks, axis=1).astype(BF16).reshape(8, 2, 16, B)
            return 0

        lax.fori_loop(0, SECTORS // 2, second_product, 0, unroll=UNROLL // 2)

    quarter = [pl.ds(4 * j, 4) for j in range(4)]
    through = {2: (0, 3), 3: (1, 2)}

    def out(i):
        target = i // 2

        @pl.when(own(i))
        def _():
            for k in range(2):
                src, dst = x_bufs[i + 1].at[:, k], out_terms.at[me.y, k]
                direct = me.y != target
                if target in through and k == 1:
                    far, between = through[target]
                    direct = jnp.logical_and(direct, me.y != far)

                    @pl.when(me.y == far)
                    def _():
                        for j in range(4):
                            remote(
                                x_bufs[i + 1].at[quarter[j], k], relay_buf.at[quarter[j]],
                                relay_s.at[0, j], relay_r.at[0, j], me.row(between),
                            ).start()

                @pl.when(me.y == target)
                def _():
                    pltpu.make_async_copy(src, dst, out_r.at[me.y, k]).start()

                @pl.when(direct)
                def _():
                    remote(src, dst, out_s.at[target, k], out_r.at[me.y, k], me.row(target)).start()

    def pass_out(target):
        far, between = through[target]

        @pl.when(me.y == between)
        def _():
            for j in range(4):
                part = relay_buf.at[quarter[j]]
                arrival(part, relay_r.at[0, j])
                remote(
                    part, out_terms.at[far, 1, quarter[j]], relay_s.at[1, j], relay_r.at[1, j], me.row(target)
                ).start()

    def h1(i):
        @pl.when(own(i))
        def _():
            remote(h_bufs[i].at[:, 1 - me.c], core_buf.at[i // 2], h1_s.at[i // 2], h1_r.at[i // 2], me.sibling()).start()

    def h2(i):
        n = i // 2

        @pl.when(own(i))
        def _():
            arrival(core_buf.at[n], h1_r.at[n])
            for g in range(8):
                part_buf[n, g] = (
                    h_bufs[i][g, me.c].astype(F32) + core_buf[n, g].astype(F32)
                ).astype(BF16)
            for g in range(8):
                @pl.when(g_me != g)
                def _():
                    remote(part_buf.at[n, g], ring_buf.at[n, g_me], h2_s.at[n, g], h2_r.at[n, g_me], me.group(g)).start()

    def h3(i):
        n = i // 2

        @pl.when(own(i))
        def _():
            total = part_buf[n, g_me].astype(F32)
            for d in range(1, 8):
                g = lax.rem(g_me + d, 8)
                arrival(ring_buf.at[n, g], h2_r.at[n, g])
                total = total + ring_buf[n, g].astype(F32)
            final_buf[n] = total.astype(BF16)

            @pl.when(me.y == n)
            def _():
                pltpu.make_async_copy(final_buf.at[n], out_block.at[me.y], h3_r.at[me.y]).start()

            @pl.when(me.y != n)
            def _():
                remote(final_buf.at[n], out_block.at[me.y], h3_s.at[n], h3_r.at[me.y], me.row(n)).start()

    def ahead(stage, i):
        if i < SITES:
            stage(i)

    p1(0)
    for d in range(1, SITES):
        site = lax.rem(me.site + d, SITES)
        arrival(ints_all.at[site], param_r.at[0, site])
        arrival(floats_all.at[site], param_r.at[1, site])
    to_smem = [
        pltpu.make_async_copy(ints_all, ints, param_l.at[0]),
        pltpu.make_async_copy(floats_all, floats, param_l.at[1]),
    ]
    for copy in to_smem:
        copy.start()
    p1(1)
    p2(0)
    for copy in to_smem + env_copies[1:]:
        copy.wait()
    p1(2)
    p2(1)
    p3(0)
    for i in range(SITES):
        ahead(p2, i + 2)
        ahead(p1, i + 3)

        def before():
            p4(i)
            multiply_first(i)

        pl.when(wanted(i))(before)
        ahead(p3, i + 1)
        if i >= 1:
            h2(i - 1)
        pl.when(wanted(i))(lambda: multiply_second(i))
        out(i)
        h1(i)
        if i == SITES - 2:
            pass_out(2)
        if i >= 2:
            h3(i - 2)
    pass_out(3)
    h2(SITES - 1)
    h3(SITES - 2)
    h3(SITES - 1)

    for q in range(ROOTS):
        for k in range(2):
            relayed = [target for target in through if k == 1 and through[target][0] == q]
            for target in relayed:
                @pl.when(me.y != target)
                def _():
                    arrival(out_terms.at[q, k], out_r.at[q, k])

                @pl.when(me.y == target)
                def _():
                    for j in range(4):
                        arrival(out_terms.at[q, k, quarter[j]], relay_r.at[1, j])
            if not relayed:
                arrival(out_terms.at[q, k], out_r.at[q, k])
        arrival(out_block.at[q], h3_r.at[q])
    for copy in sends:
        copy.wait_send()

    def left(src, sem):
        pltpu.make_async_copy(src, src, sem).wait()

    for i in range(SITES):
        a = a_bufs[i]

        @pl.when(me.site == i)
        def _():
            for d in (1, 2, 3):
                for parts, sem in ((first_parts, ya_s), (second_parts, yb_s)):
                    for src, dst, n in parts(0, i):
                        left(dst, sem.at[d, n])

        @pl.when(own(i))
        def _():
            if i < EARLY:
                for d in (1, 2, 3):
                    left(a.at[0, 0, 0, first], za_s.at[i, d - 1])
            for n in range(1 if i == last else 3):
                left(a.at[0, 0, 0, first], xa_s.at[i, n])
            for n in range(1 if i == last else 3):
                left(a.at[0, :, 0, second], xb_s.at[i, n])
            left(core_buf.at[i // 2], h1_s.at[i // 2])
            for g in range(8):
                @pl.when(g_me != g)
                def _():
                    left(part_buf.at[i // 2, g], h2_s.at[i // 2, g])

            @pl.when(me.y != i // 2)
            def _():
                for k in range(2):
                    if i // 2 in through and k == 1:
                        @pl.when(me.y != through[i // 2][0])
                        def _():
                            left(x_bufs[i + 1].at[:, k], out_s.at[i // 2, k])
                    else:
                        left(x_bufs[i + 1].at[:, k], out_s.at[i // 2, k])
                left(final_buf.at[i // 2], h3_s.at[i // 2])

        @pl.when(wanted(i))
        def _():
            for d in (1, 2, 3):
                left(a.at[:, 0, 0, first], zb_s.at[i, d - 1])
            left(a.at[:, :, 0], c_s.at[i])
    for n, low in ((0, 0), (1, 2)):
        @pl.when(jnp.logical_or(me.y == low, me.y == low + 1))
        def _():
            for j in range(4):
                left(relay_buf.at[quarter[j]], relay_s.at[n, j])


def shards(mps, sector_map, live_rows, term_mask, term_coef, block_coef, env_terms, env_block):
    dma = pltpu.SemaphoreType.DMA
    vmem = pltpu.VMEM
    scratch = [vmem((2, 4, 2, STATES, B, B), BF16)] * SITES
    scratch += [vmem((SECTORS, CHAINS, B, B), BF16)] * (SITES + 1)
    scratch += [vmem((8, 2, 8, 16, B), BF16)] * SITES
    scratch += [
        vmem((SECTORS, STATES, B, CHAINS * B), BF16),
        vmem((4, 8, 8, 16, B), BF16),
        vmem((4, 8, 8, 16, B), BF16),
        vmem((4, 8, 8, 16, B), BF16),
        vmem((4, 8, 16, B), BF16),
        vmem((SITES, 24, B), jnp.int32),
        vmem((SITES, 8, B), F32),
        pltpu.SMEM((SITES, 24, B), jnp.int32),
        pltpu.SMEM((SITES, 8, B), F32),
        vmem((8, 16, B), BF16),
        vmem((SECTORS, B, B), BF16),
        dma((2, SITES)), dma((2, SITES)), dma((2,)),
        dma((4, 1)), dma((4, 1)), dma((4, 2)), dma((4, 2)),
        dma((SITES, 3)), dma((SITES, 2)),
        dma((SITES, 3)), dma((SITES, 4)),
        dma((SITES, 3)), dma((SITES, 2)),
        dma((SITES, 3)), dma((SITES, 4)),
        dma((SITES,)), dma((SITES,)),
        dma((3,)),
        dma((4, 2)), dma((4, 2)),
        dma((2, 4)), dma((2, 4)),
        dma((4,)), dma((4,)),
        dma((4, 8)), dma((4, 8)),
        dma((4,)), dma((4,)),
    ]
    anywhere = pl.BlockSpec(memory_space=pl.ANY)
    inside = pl.BlockSpec(memory_space=pltpu.VMEM)
    terms, block = pl.pallas_call(
        kernel,
        out_shape=(
            jax.ShapeDtypeStruct((ROOTS, 2, SECTORS, B, B), BF16),
            jax.ShapeDtypeStruct((ROOTS, 8, 16, B), BF16),
        ),
        in_specs=[inside] * 5 + [anywhere] * 3,
        out_specs=(anywhere, anywhere),
        scratch_shapes=scratch,
        compiler_params=pltpu.CompilerParams(
            collective_id=0, has_side_effects=True, vmem_limit_bytes=56 * 2**20
        ),
        name="chains",
    )(
        sector_map[0], live_rows, term_mask[0], term_coef[0], block_coef,
        env_block.reshape(ROOTS, 8, 16, B), mps[0].reshape(ROOTS, STATES, 2, 4, 2, B, B), env_terms,
    )
    return terms[None], block.reshape(1, ROOTS, SECTORS, 8, B)


def solution(mesh):
    in_specs = (
        P("site", None, None, None, None, None),
        P("site", None, None),
        P("site", None),
        P("site", "op", None),
        P("site", "op", None),
        P("site", "op"),
        P(None, "op", None, None, None),
        P(None, None, "op", None),
    )
    out_specs = (P("site", None, "op", None, None, None), P("site", None, None, "op", None))
    return jax.shard_map(shards, mesh=mesh, in_specs=in_specs, out_specs=out_specs, check_vma=False)
```

time: 156 us -> 142 us (0.910)
  Pallas kernels: 142 us -> 135 us
  other arithmetic: 5.57 us -> 0 us
    pallas_call x1, Pallas kernels: 142 us -> 135 us  [shards(): pl.pallas_call(kernel, out_shape=(jax.ShapeDtypeStruct((ROOTS, 2, SECTORS...]
    reshape x2 -> x0, other arithmetic: 2.65 us -> none  [the longest x1 1.33 us: shards(): ints.reshape(8, B)]
where the time goes in v2:
time: 142 us
  Pallas kernels  135 us (95%)
  local copies, waits for them, and re-layouts  5.48 us (4%)
    pallas_call x1, Pallas kernels, shards(): pl.pallas_call(kernel, out_shape=(jax.ShapeDtypeStruct((ROOTS, 2, SECTORS...  135 us
    unnamed x4, local copies, waits for them, and re-layouts  5.48 us

profile of v2, /device:TPU:28, one launch (start us, length us, event | category | flops | bytes accessed | tf_op | source)
XLA Modules:
  0.0 141.6 jit_solution(5559350396930834106)
XLA Ops:
  0.6 135.4 %chains.1 = (bf16[4,2,16,128,128]{4,3,2,1,0:T(8,128)(2,1)}, bf16[4,8,16,128]{3,2,1,0:T(8,128)(2,1)}) custom-call(s32[4,16]{1,0:T(4,128)} %bitcast.11, s32[1,16]{1,0:T(1,128)} %live_ref.1, s32[2,4]{1,0:T(2,128)} %bitcast.12, f32[2,4]{1,0:T(2,128)} %bitcast.13, f32[1,2]{1,0:T(1,128)} %pair_ref.1, bf16[4,8,16,128]{3,2,1,0:T(8,128)(2,1)} %bitcast.9, ...), custom_call_target="tpu_custom_call" | custom-call | tf_op jit(solution)/shard_map/chains/pallas_call | solution.py:516
  136.1 0.0 copy-start
  136.1 4.8 %copy.12 = bf16[1,4,2,16,128,128]{5,4,3,2,1,0:T(8,128)(2,1)} copy(bf16[1,4,2,16,128,128]{5,4,3,2,1,0:T(8,128)(2,1)} %bitcast.8) | data formatting | bytes 8388608
  140.9 0.0 copy-done
  140.9 0.7 copy.13
Async XLA Ops:
  136.1 4.8 %copy-start = (bf16[4,8,16,128]{3,2,1,0:T(8,128)(2,1)S(1)}, bf16[4,8,16,128]{3,2,1,0:T(8,128)(2,1)}, u32[]{:S(2)}) copy-start(bf16[4,8,16,128]{3,2,1,0:T(8,128)(2,1)} %get-tuple-element.5) | copy-start | bytes 393220

commit v3 on v2

--- a/solution.py
+++ b/solution.py
@@ -177,6 +177,10 @@
                 arrival(part, yb_r.at[i // 2, 0])
                 for d in (1, 3, 2):
                     remote(part, part, za_s.at[i, d - 1], za_r.at[i, me.z], me.along_z(d)).start()
+            else:
+                for n in range(2):
+                    arrival(a.at[me.l, :, me.c, 2 + n], yb_r.at[i // 2, n])
+                send_second(i)
 
     def p2(i):
         a = a_bufs[i]
@@ -187,10 +191,7 @@
                 for d in (1, 3, 2):
                     z = lax.rem(me.z + d, 4)
                     arrival(a.at[me.l, z, me.c, second], za_r.at[i, z])
-            else:
-                for n in range(2):
-                    arrival(a.at[me.l, :, me.c, 2 + n], yb_r.at[i // 2, n])
-            send_second(i)
+                send_second(i)
 
         @pl.when(wanted(i))
         def _():
@@ -523,7 +524,7 @@
         out_specs=(anywhere, anywhere),
         scratch_shapes=scratch,
         compiler_params=pltpu.CompilerParams(
-            collective_id=0, has_side_effects=True, vmem_limit_bytes=56 * 2**20
+            collective_id=0, has_side_effects=True, vmem_limit_bytes=46 * 2**20
         ),
         name="chains",
     )(

time: 142 us -> 142 us (level)
  local copies, waits for them, and re-layouts: 5.48 us -> 6.92 us
    pallas_call x1, Pallas kernels: 135 us -> 134 us  [shards(): pl.pallas_call(kernel, out_shape=(jax.ShapeDtypeStruct((ROOTS, 2, SECTORS...]
    unnamed x4 -> x14, local copies, waits for them, and re-layouts: 5.48 us -> 6.92 us
where the time goes in v3:
time: 142 us; the launch traced here: 141 us
  Pallas kernels  134 us (94%)
  local copies, waits for them, and re-layouts  6.92 us (5%)
    pallas_call x1, Pallas kernels, shards(): pl.pallas_call(kernel, out_shape=(jax.ShapeDtypeStruct((ROOTS, 2, SECTORS...  134 us
    unnamed x14, local copies, waits for them, and re-layouts  6.92 us

profile of v3, /device:TPU:28, one launch (start us, length us, event | category | flops | bytes accessed | tf_op | source)
XLA Modules:
  0.0 141.5 jit_solution(2705660632602035410)
XLA Ops:
  0.6 0.0 copy-start
  0.6 0.9 copy-done
  1.5 0.0 copy-start.1
  1.5 0.7 copy-done.1
  2.2 0.0 copy-start.2
  2.2 0.7 copy-done.2
  2.9 0.0 copy-start.3
  2.9 0.7 copy-done.3
  3.6 0.0 copy-start.4
  3.6 0.7 copy-done.4
  4.2 0.0 copy-start.5
  4.2 0.7 copy-done.5
  4.9 133.9 %chains.1 = (bf16[4,2,16,128,128]{4,3,2,1,0:T(8,128)(2,1)S(1)}, bf16[4,8,16,128]{3,2,1,0:T(8,128)(2,1)S(1)}) custom-call(s32[4,16]{1,0:T(4,128)S(1)} %bitcast.10, s32[1,16]{1,0:T(1,128)S(1)} %copy-done.4, s32[2,4]{1,0:T(2,128)S(1)} %bitcast.11, f32[2,4]{1,0:T(2,128)S(1)} %bitcast.12, f32[1,2]{1,0:T(1,128)S(1)} %copy-done.5, ...), custom_call_target="tpu_custom_call" | custom-call | tf_op jit(solution)/shard_map/chains/pallas_call | solution.py:517
  138.8 2.0 %copy.12 = bf16[1,4,2,16,128,128]{5,4,3,2,1,0:T(8,128)(2,1)} copy(bf16[1,4,2,16,128,128]{5,4,3,2,1,0:T(8,128)(2,1)S(1)} %bitcast.7) | data formatting | bytes 8388608
  140.8 0.7 copy.13
Async XLA Ops:
  0.6 0.9 copy-start
  1.5 0.7 copy-start.1
  2.2 0.7 copy-start.2
  2.9 0.7 copy-start.3
  3.6 0.7 copy-start.4
  4.2 0.7 copy-start.5
